TPU v7x, 256 devices: a whole 4x4x8 slice. The times are simulated.
256 devices in a mesh: ctx: 16 (over x, z_lo), tp: 4 (over z_hi, core), dp: 4 (over y).
Axes of the slice: x: 4, y: 4, z: 8 (z_hi: 2, z_lo: 4; z = z_hi * 4 + z_lo), core: 2. Of those that a mesh axis runs over, the one named last changes fastest.
Arguments:
- trailing_questions: bfloat16 [8192, 8192], P(('dp', 'ctx'), 'tp'), parts along dimension 0, may hold values from -6 to 6
- output_gradient: bfloat16 [8192, 8192], P(('dp', 'ctx'), 'tp'), parts along dimension 0, may hold values from -6 to 6
- tail_row_key: bfloat16 [8192, 1024], P(('dp', 'ctx'), 'tp'), parts along dimension 0, may hold values from -6 to 6
- tail_row_value: bfloat16 [8192, 1024], P(('dp', 'ctx'), 'tp'), parts along dimension 0, may hold values from -6 to 6
- passage_key_cache: bfloat16 [16384, 1024], P(('dp', 'ctx'), 'tp'), parts along dimension 0, may hold values from -6 to 6
- passage_value_cache: bfloat16 [16384, 1024], P(('dp', 'ctx'), 'tp'), parts along dimension 0, may hold values from -6 to 6
- row_list: int32 [8192], P(('dp', 'ctx')), parts along dimension 0, may hold values from 0 to 1, as said below
- read_owner: int32 [64, 24], P(('dp', 'ctx')), parts along dimension 0, may hold values from 0 to 15, as said below
- read_tile: int32 [64, 24], P(('dp', 'ctx')), parts along dimension 0, may hold values from 0 to 1
- read_list: int32 [64, 24], P(('dp', 'ctx')), parts along dimension 0, may hold values from 0 to 1
- read_count: int32 [64], P(('dp', 'ctx')), parts along dimension 0, may hold values from 12 to 24, as said below
Outputs:
- grad_query: bfloat16 [8192, 8192], P(('dp', 'ctx'), 'tp'), parts along dimension 0
- grad_tail_key: bfloat16 [8192, 1024], P(('dp', 'ctx'), 'tp'), parts along dimension 0
- grad_tail_value: bfloat16 [8192, 1024], P(('dp', 'ctx'), 'tp'), parts along dimension 0
- grad_key_cache: float32 [16384, 1024], P(('dp', 'ctx'), 'tp'), parts along dimension 0
- grad_value_cache: float32 [16384, 1024], P(('dp', 'ctx'), 'tp'), parts along dimension 0
There are 4 independent parts, one for each index of `dp`. A program takes and returns all parts, laid end to end along the dimension named above; each array names one. Nothing has to cross between parts.
Inputs may be any that keep to these rules, and one draw needn't show every extreme that they name: `row_list`: on each reader's 128 rows the list number is 0 on a first run and 1 on the rest; both runs are nonempty. `read_owner`: a reader names one owner at most 2 times, and every reader names some owner exactly 2 times. `read_count`: some reader has all 24 reads live.
All inputs are finite; a program needn't handle non-finite values.
Results may differ from a plain program's by a relative error of at most 0.012.
Values may be sent and summed in bfloat16 or wider, within the bound.
A program may use at most 64 MiB of HBM per device.

v0:
```python
import functools
import math

import jax
import jax.numpy as jnp
from jax import lax
from jax.experimental import pallas as pl
from jax.experimental.pallas import tpu as pltpu
from jax.sharding import PartitionSpec as P

W = 128
NX = 4
NZ = 4
SCALE = 1.0 / math.sqrt(W)
LOG2E = 1.4426950408889634
SCORE_TO_LOG2 = SCALE * LOG2E
MASKED = -1e30
FLOOR = -1e29
NB = 256
f32 = jnp.float32
bf16 = jnp.bfloat16
MESH = pl.DeviceIdType.MESH
TT = (((0,), (0,)), ((), ()))


def kernel(
    q_ref, do_ref, tk_ref, tv_ref, kc_ref, vc_ref, rl_ref, ro_ref, rt_ref, rs_ref, rc_ref,
    gq_ref, gk_ref, gv_ref, gck_ref, gcv_ref,
    G, GR, R1, R2, RZ2, RZ, QR, DR, QT, DT, m_ref, l_ref, c_ref, bias_ref, dq_ref, pb, db,
    a_recv, a_send_x, a_send_zi, a_send_zo,
    r1_recv, r1_send, r2_recv, r2_send, rz2_recv, rz2_send, rz_recv, rz_send,
):
    me = lax.axis_index("ctx")
    x = me // NZ
    z = me % NZ
    xp = lax.rem(x + 1, NX)
    xm = lax.rem(x + NX - 1, NX)
    x2 = lax.rem(x + 2, NX)
    inner = (z == 1) | (z == 2)
    edge = (z == 0) | (z == 3)
    low = z < 2
    zi = jnp.where(low, z + 1, z - 1)
    zo = jnp.where(low, z - 1, z + 1)
    to_xp = xp * NZ + z
    to_xm = xm * NZ + z
    to_zi = x * NZ + zi
    to_zo = x * NZ + zo
    zk = [z, jnp.where(lax.rem(z, 2) == 0, z + 1, z - 1), jnp.where(low, 2, 1), jnp.where(low, 3, 0)]

    def when(cond, fn):
        if cond is None:
            fn()
        else:
            pl.when(cond)(fn)

    def send(src, dst, ssem, rsem, dev):
        pltpu.make_async_remote_copy(
            src_ref=src, dst_ref=dst, send_sem=ssem, recv_sem=rsem, device_id={"ctx": dev}, device_id_type=MESH
        ).start()

    def wait_recv(dst, rsem):
        pltpu.make_async_remote_copy(
            src_ref=dst, dst_ref=dst, send_sem=rsem, recv_sem=rsem, device_id={"ctx": to_xp}, device_id_type=MESH
        ).wait_recv()

    def wait_send(src, ssem):
        pltpu.make_async_remote_copy(
            src_ref=src, dst_ref=src, send_sem=ssem, recv_sem=ssem, device_id={"ctx": to_xp}, device_id_type=MESH
        ).wait_send()

    barrier = pltpu.get_barrier_semaphore()

    def greet(dev):
        pl.semaphore_signal(barrier, inc=1, device_id={"ctx": dev}, device_id_type=MESH)

    greet(to_xp)
    greet(to_xm)
    greet(to_zi)
    when(inner, lambda: greet(to_zo))

    for a in range(2):
        G[me, a, 0] = kc_ref[a * W : (a + 1) * W, :]
        G[me, a, 1] = vc_ref[a * W : (a + 1) * W, :]

    when(inner, lambda: pl.semaphore_wait(barrier, 4))
    when(edge, lambda: pl.semaphore_wait(barrier, 3))

    def a_x(owner, k, a, dirs=(0, 1), slot=None):
        for d in dirs:
            send(
                G.at[owner, a], G.at[owner, a], a_send_x.at[d, k, a if slot is None else slot], a_recv.at[owner, a],
                (to_xp, to_xm)[d],
            )

    def a_zi(owner, k, a):
        send(G.at[owner, a], G.at[owner, a], a_send_zi.at[k, a], a_recv.at[owner, a], to_zi)

    def a_zo(owner, k, a):
        send(G.at[owner, a], G.at[owner, a], a_send_zo.at[k, a], a_recv.at[owner, a], to_zo)

    for a in range(2):
        a_zi(me, 0, a)
        when(inner, functools.partial(a_zo, me, 0, a))
        a_x(me, 0, a)

    for h in range(2):
        for j in range(8):
            cols = slice((h * 8 + j) * W, (h * 8 + j + 1) * W)
            rows = slice(j * W, (j + 1) * W)
            qb = q_ref[:, cols]
            ob = do_ref[:, cols]
            QR[h, rows, :] = qb
            DR[h, rows, :] = ob
            QT[h, :, rows] = qb.T
            DT[h, :, rows] = ob.T
    reads = ro_ref.shape[1]
    tid = ro_ref[...] * 2 + rt_ref[...]
    live = lax.broadcasted_iota(jnp.int32, (1, reads), 1) < rc_ref[...]
    tid = jnp.where(live, tid, -1)
    named = lax.broadcasted_iota(jnp.int32, (2 * NX * NZ, reads), 0) == tid
    count0 = jnp.sum(jnp.where(named & (rs_ref[...] == 0), 1.0, 0.0), axis=1, keepdims=True)
    count1 = jnp.sum(jnp.where(named & (rs_ref[...] == 1), 1.0, 0.0), axis=1, keepdims=True)
    rl = rl_ref[...]
    times = jnp.where(rl == 0, count0, count1)
    bias_ref[...] = jnp.where(times > 0.5, jnp.log2(jnp.maximum(times, 1.0)), MASKED)
    cut = jnp.sum(jnp.where(rl == 0, 1.0, 0.0), axis=1, keepdims=True)
    key_at = lax.broadcasted_iota(jnp.int32, (W, W), 0)
    row_at = lax.broadcasted_iota(jnp.int32, (W, W), 1)
    tail_ok = (key_at <= row_at) & jnp.logical_not((key_at.astype(f32) < cut) & (row_at.astype(f32) >= cut))
    tail_ok = jnp.concatenate([tail_ok.astype(f32)] * (NB // W), axis=1) > 0.5

    for h in range(2):
        hs = slice(h * W, (h + 1) * W)
        for j in range(8 * W // NB):
            sl = slice(j * NB, (j + 1) * NB)
            s = jnp.dot(tk_ref[:, hs], QT[h, :, sl], preferred_element_type=f32)
            dp = jnp.dot(tv_ref[:, hs], DT[h, :, sl], preferred_element_type=f32)
            t = jnp.where(tail_ok, s * SCORE_TO_LOG2, MASKED).reshape(16, 8, NB)
            top = jnp.maximum(jnp.max(t, axis=0), FLOOR)
            e = jnp.exp2(t - top[None])
            m_ref[h, :, sl] = top
            l_ref[h, :, sl] = jnp.sum(e, axis=0)
            c_ref[h, :, sl] = jnp.sum(e * dp.reshape(16, 8, NB), axis=0)

    def tile_bias(owner, a):
        b = jnp.broadcast_to(bias_ref[pl.ds(owner * 2 + a, 1), :], (8, W))
        return jnp.concatenate([b] * (NB // W), axis=1)

    def stats_chunk(owner):
        for a in range(2):
            b = tile_bias(owner, a)
            for h in range(2):
                hs = slice(h * W, (h + 1) * W)
                for j in range(8 * W // NB):
                    sl = slice(j * NB, (j + 1) * NB)
                    s = jnp.dot(G[owner, a, 0, :, hs], QT[h, :, sl], preferred_element_type=f32)
                    dp = jnp.dot(G[owner, a, 1, :, hs], DT[h, :, sl], preferred_element_type=f32)
                    t = (s * SCORE_TO_LOG2).reshape(16, 8, NB)
                    old = m_ref[h, :, sl]
                    new = jnp.maximum(old, jnp.max(t, axis=0) + b)
                    fade = jnp.exp2(old - new)
                    e = jnp.exp2(t - (new - b)[None])
                    m_ref[h, :, sl] = new
                    l_ref[h, :, sl] = l_ref[h, :, sl] * fade + jnp.sum(e, axis=0)
                    c_ref[h, :, sl] = c_ref[h, :, sl] * fade + jnp.sum(e * dp.reshape(16, 8, NB), axis=0)

    def got_a(k):
        owner = x * NZ + zk[k]
        for a in range(2):
            wait_recv(G.at[owner, a], a_recv.at[owner, a])
            when(inner, functools.partial(a_zi if k == 1 else a_zo, owner, k, a))
            a_x(owner, k, a)

    def got_b(k):
        right = xp * NZ + zk[k]
        left = xm * NZ + zk[k]
        wait_recv(G.at[left, 0], a_recv.at[left, 0])
        if k < 2:
            a_x(left, k, 0, (0,), 2)
        wait_recv(G.at[right, 0], a_recv.at[right, 0])
        wait_recv(G.at[right, 1], a_recv.at[right, 1])
        if k < 2:
            a_x(right, k, 1, (1,), 2)
        wait_recv(G.at[left, 1], a_recv.at[left, 1])

    def got_c(k):
        owner = x2 * NZ + zk[k]
        for a in range(2):
            wait_recv(G.at[owner, a], a_recv.at[owner, a])
            if k < 2:
                when(inner, functools.partial(a_zi, owner, k + 2, a))
            else:
                when(inner, functools.partial(a_zo, owner, k + 2, a))

    gather_plan = [
        (x * NZ + zk[0], None),
        (x * NZ + zk[1], lambda: got_a(1)),
        (xp * NZ + zk[0], lambda: got_b(0)),
        (xm * NZ + zk[0], None),
        (x * NZ + zk[2], lambda: got_a(2)),
        (xp * NZ + zk[1], lambda: got_b(1)),
        (xm * NZ + zk[1], None),
        (x2 * NZ + zk[0], lambda: got_c(0)),
        (x * NZ + zk[3], lambda: got_a(3)),
        (x2 * NZ + zk[1], lambda: got_c(1)),
        (xp * NZ + zk[2], lambda: got_b(2)),
        (xm * NZ + zk[2], None),
        (xp * NZ + zk[3], lambda: got_b(3)),
        (xm * NZ + zk[3], None),
        (x2 * NZ + zk[2], lambda: got_c(2)),
        (x2 * NZ + zk[3], lambda: got_c(3)),
    ]

    def gather_step(n, carry):
        owner = jnp.int32(0)
        for at, (own, act) in enumerate(gather_plan):
            owner = jnp.where(n == at, own, owner)
            if act is not None:
                pl.when(n == at)(act)
        stats_chunk(owner)
        return carry

    lax.fori_loop(0, len(gather_plan), gather_step, 0)

    for h in range(2):
        m = m_ref[h]
        top = jnp.max(m, axis=0, keepdims=True)
        part = jnp.exp2(m - top)
        total = jnp.sum(l_ref[h] * part, axis=0, keepdims=True)
        cross = jnp.sum(c_ref[h] * part, axis=0, keepdims=True)
        m_ref[h] = jnp.broadcast_to(top + jnp.log2(total), (8, 8 * W))
        c_ref[h] = jnp.broadcast_to(cross / total, (8, 8 * W))
        dq_ref[h] = jnp.zeros((W, 8 * W), f32)

    def grads_chunk(owner):
        for h in range(2):
            hs = slice(h * W, (h + 1) * W)
            for a in range(2):
                b = tile_bias(owner, a)
                rows = slice(a * W, (a + 1) * W)
                for j in range(8 * W // NB):
                    sl = slice(j * NB, (j + 1) * NB)
                    s = jnp.dot(G[owner, a, 0, :, hs], QT[h, :, sl], preferred_element_type=f32)
                    dp = jnp.dot(G[owner, a, 1, :, hs], DT[h, :, sl], preferred_element_type=f32)
                    p = jnp.exp2((s * SCORE_TO_LOG2).reshape(16, 8, NB) - (m_ref[h, :, sl] - b)[None])
                    d = p * (dp.reshape(16, 8, NB) - c_ref[h, :, sl][None])
                    pb[h, rows, sl] = p.reshape(W, NB).astype(bf16)
                    db[h, rows, sl] = d.reshape(W, NB).astype(bf16)
            dv = jnp.dot(pb[h], DR[h], preferred_element_type=f32)
            dk = jnp.dot(db[h], QR[h], preferred_element_type=f32) * SCALE
            for a in range(2):
                rows = slice(a * W, (a + 1) * W)
                GR[owner, a, 0, :, hs] = dk[rows].astype(bf16)
                GR[owner, a, 1, :, hs] = dv[rows].astype(bf16)
            keys = jnp.concatenate([G[owner, 0, 0, :, hs], G[owner, 1, 0, :, hs]], axis=0)
            dq_ref[h] += lax.dot_general(keys, db[h], TT, preferred_element_type=f32)

    def merge(ref, parts):
        def rows_of(i, carry):
            r = pl.ds(pl.multiple_of(i * 32, 32), 32)
            total = ref[:, r, :].astype(f32)
            for part in parts:
                total = total + part[:, r, :].astype(f32)
            ref[:, r, :] = total.astype(bf16)
            return carry

        lax.fori_loop(0, W // 32, rows_of, 0)

    def r1(d, k, a):
        owner = (xm if d == 0 else xp) * NZ + zk[k]
        send(GR.at[owner, a], R1.at[d, k, a], r1_send.at[d, k, a], r1_recv.at[d, k, a], (to_xm, to_xp)[d])

    def r1_both(d, k):
        r1(d, k, 0)
        r1(d, k, 1)

    def r2(k):
        owner = x2 * NZ + zk[k]
        for a in range(2):
            send(GR.at[owner, a], R2.at[k, a], r2_send.at[k, a], r2_recv.at[k, a], (to_xm, to_xp)[a])

    def r2_merged(k):
        def fn():
            owner = x2 * NZ + zk[k]
            for a in range(2):
                wait_recv(RZ2.at[k, a], rz2_recv.at[k, a])
                merge(GR.at[owner, a], [RZ2.at[k, a]])
            r2(k)

        return fn

    def rz2_edge(k):
        def fn():
            owner = x2 * NZ + zk[k]
            for a in range(2):
                send(GR.at[owner, a], RZ2.at[k, a], rz2_send.at[k - 2, a], rz2_recv.at[k, a], to_zi)

        return fn

    def rz2_inner(k):
        def fn():
            owner = x2 * NZ + zk[k]
            for a in range(2):
                wait_recv(RZ2.at[k, a], rz2_recv.at[k, a])
                merge(GR.at[owner, a], [RZ2.at[k, a]])
                send(GR.at[owner, a], RZ2.at[k - 2, a], rz2_send.at[k - 2, a], rz2_recv.at[k - 2, a], to_zi)

        return fn

    def r1_merged(k):
        for d in range(2):
            a = d
            owner = (xm if d == 0 else xp) * NZ + zk[k]
            wait_recv(R2.at[k, a], r2_recv.at[k, a])
            merge(GR.at[owner, a], [R2.at[k, a]])
            r1(d, k, a)

    def got_r1(k, a):
        for d in range(2):
            wait_recv(R1.at[d, k, a], r1_recv.at[d, k, a])

    def rz_edge(k):
        def fn():
            owner = x * NZ + zk[k]
            slot = 4 if k == 1 else k
            for a in range(2):
                got_r1(k, a)
                merge(GR.at[owner, a], [R1.at[0, k, a], R1.at[1, k, a]])
                send(GR.at[owner, a], RZ.at[slot, a], rz_send.at[k - 1, a], rz_recv.at[slot, a], to_zi)

        return fn

    def rz_inner(k):
        def fn():
            owner = x * NZ + zk[k]
            slot = 0 if k == 1 else k - 2
            for a in range(2):
                got_r1(k, a)
                wait_recv(RZ.at[k, a], rz_recv.at[k, a])
                merge(GR.at[owner, a], [R1.at[0, k, a], R1.at[1, k, a], RZ.at[k, a]])
                send(GR.at[owner, a], RZ.at[slot, a], rz_send.at[k - 1, a], rz_recv.at[slot, a], to_zo if k == 1 else to_zi)

        return fn

    plan = {n: [] for n in range(16)}
    plan[0] += [(edge, rz2_edge(3))]
    plan[1] += [(None, lambda: r1_both(0, 3))]
    plan[2] += [(None, lambda: r1_both(1, 3))]
    plan[4] += [(edge, rz2_edge(2))]
    plan[5] += [(None, lambda: r1_both(0, 2)), (inner, rz2_inner(3))]
    plan[6] += [(None, lambda: r1_both(1, 2))]
    plan[7] += [(edge, rz_edge(3))]
    plan[8] += [(edge, lambda: r2(1)), (inner, rz2_inner(2))]
    plan[9] += [(None, lambda: r1(0, 1, 1))]
    plan[10] += [(None, lambda: r1(1, 1, 0)), (inner, r2_merged(1))]
    plan[11] += [(edge, rz_edge(2)), (inner, rz_inner(3))]
    plan[12] += [(edge, lambda: r2(0)), (None, lambda: r1_merged(1))]
    plan[13] += [(None, lambda: r1(0, 0, 1)), (inner, r2_merged(0))]
    plan[14] += [(None, lambda: r1(1, 0, 0)), (inner, rz_inner(2))]
    plan[15] += [(None, lambda: r1_merged(0))]

    def scatter_step(n, carry):
        kind = lax.rem(n, 4)
        at = n // 4
        zs = jnp.where(at == 0, zk[3], jnp.where(at == 1, zk[2], jnp.where(at == 2, zk[1], zk[0])))
        xs = jnp.where(kind == 0, x2, jnp.where(kind == 1, xm, jnp.where(kind == 2, xp, x)))
        grads_chunk(xs * NZ + zs)
        for step, acts in plan.items():
            if acts:

                def run(acts=acts):
                    for cond, act in acts:
                        when(cond, act)

                pl.when(n == step)(run)
        return carry

    lax.fori_loop(0, 16, scatter_step, 0)

    for h in range(2):
        hs = slice(h * W, (h + 1) * W)
        for j in range(8 * W // NB):
            sl = slice(j * NB, (j + 1) * NB)
            s = jnp.dot(tk_ref[:, hs], QT[h, :, sl], preferred_element_type=f32)
            dp = jnp.dot(tv_ref[:, hs], DT[h, :, sl], preferred_element_type=f32)
            t = jnp.where(tail_ok, s * SCORE_TO_LOG2, MASKED).reshape(16, 8, NB)
            p = jnp.exp2(t - m_ref[h, :, sl][None])
            d = p * (dp.reshape(16, 8, NB) - c_ref[h, :, sl][None])
            pb[h, :W, sl] = p.reshape(W, NB).astype(bf16)
            db[h, :W, sl] = d.reshape(W, NB).astype(bf16)
        gv_ref[:, hs] = jnp.dot(pb[h, :W, :], DR[h], preferred_element_type=f32).astype(bf16)
        gk_ref[:, hs] = (jnp.dot(db[h, :W, :], QR[h], preferred_element_type=f32) * SCALE).astype(bf16)
        dq_ref[h] += lax.dot_general(tk_ref[:, hs], db[h, :W, :], TT, preferred_element_type=f32)

    when(edge, rz_edge(1))
    when(inner, rz_inner(1))

    for h in range(2):
        for j in range(8):
            gq_ref[:, (h * 8 + j) * W : (h * 8 + j + 1) * W] = (
                (dq_ref[h, :, j * W : (j + 1) * W] * SCALE).T.astype(bf16)
            )

    for a in range(2):
        rows = slice(a * W, (a + 1) * W)
        got_r1(0, a)
        wait_recv(RZ.at[0, a], rz_recv.at[0, a])
        for i, out in enumerate((gck_ref, gcv_ref)):
            out[rows, :] = (
                GR[me, a, i].astype(f32)
                + R1[0, 0, a, i].astype(f32)
                + R1[1, 0, a, i].astype(f32)
                + RZ[0, a, i].astype(f32)
            )

        def add_outer(a=a, rows=rows):
            wait_recv(RZ.at[4, a], rz_recv.at[4, a])
            for i, out in enumerate((gck_ref, gcv_ref)):
                out[rows, :] += RZ[4, a, i].astype(f32)

        when(inner, add_outer)

    tile = G.at[0, 0]
    for a in range(2):
        for k in range(4):
            wait_send(tile, a_send_x.at[0, k, a])
            wait_send(tile, a_send_x.at[1, k, a])
            wait_send(tile, r1_send.at[0, k, a])
            wait_send(tile, r1_send.at[1, k, a])
        for k in range(2):
            wait_send(tile, r2_send.at[k, a])
            wait_send(tile, rz2_send.at[k, a])
            wait_send(tile, a_send_x.at[a, k, 2])
        for k in range(3):
            wait_send(tile, rz_send.at[k, a])
        wait_send(tile, a_send_zi.at[0, a])

        def inner_sends(a=a):
            for k in (1, 2, 3):
                wait_send(tile, a_send_zi.at[k, a])
            for k in (0, 2, 3, 4, 5):
                wait_send(tile, a_send_zo.at[k, a])

        when(inner, inner_sends)


def body(q, do, tk, tv, kc, vc, row_list, read_owner, read_tile, read_list, read_count):
    rows, width = q.shape
    kv_width = tk.shape[1]
    groups = width // kv_width
    vmem = pl.BlockSpec(memory_space=pltpu.VMEM)
    tile = (2, W, kv_width)
    dma = pltpu.SemaphoreType.DMA
    scratch = [
        pltpu.VMEM((NX * NZ, 2) + tile, bf16),
        pltpu.VMEM((NX * NZ, 2) + tile, bf16),
        pltpu.VMEM((2, 4, 2) + tile, bf16),
        pltpu.VMEM((2, 2) + tile, bf16),
        pltpu.VMEM((4, 2) + tile, bf16),
        pltpu.VMEM((5, 2) + tile, bf16),
        pltpu.VMEM((2, groups * W, W), bf16),
        pltpu.VMEM((2, groups * W, W), bf16),
        pltpu.VMEM((2, W, groups * W), bf16),
        pltpu.VMEM((2, W, groups * W), bf16),
        pltpu.VMEM((2, 8, groups * W), f32),
        pltpu.VMEM((2, 8, groups * W), f32),
        pltpu.VMEM((2, 8, groups * W), f32),
        pltpu.VMEM((2 * NX * NZ, W), f32),
        pltpu.VMEM((2, W, groups * W), f32),
        pltpu.VMEM((2, 2 * W, groups * W), bf16),
        pltpu.VMEM((2, 2 * W, groups * W), bf16),
        dma((NX * NZ, 2)),
        dma((2, 4, 3)),
        dma((4, 2)),
        dma((6, 2)),
        dma((2, 4, 2)),
        dma((2, 4, 2)),
        dma((2, 2)),
        dma((2, 2)),
        dma((4, 2)),
        dma((2, 2)),
        dma((5, 2)),
        dma((3, 2)),
    ]
    pairs = 2 * groups * rows * (2 * NX * NZ + 1) * W * W * 2
    return pl.pallas_call(
        kernel,
        name="tail_attention_backward",
        out_shape=(
            jax.ShapeDtypeStruct((rows, width), bf16),
            jax.ShapeDtypeStruct((rows, kv_width), bf16),
            jax.ShapeDtypeStruct((rows, kv_width), bf16),
            jax.ShapeDtypeStruct(kc.shape, f32),
            jax.ShapeDtypeStruct(vc.shape, f32),
        ),
        in_specs=[vmem] * 11,
        out_specs=(vmem,) * 5,
        scratch_shapes=scratch,
        cost_estimate=pl.CostEstimate(flops=7 * pairs, bytes_accessed=4 << 20, transcendentals=pairs // W),
        compiler_params=pltpu.CompilerParams(
            collective_id=0, has_side_effects=True, vmem_limit_bytes=48 << 20
        ),
    )(
        q, do, tk, tv, kc, vc,
        row_list.reshape(1, rows), read_owner, read_tile, read_list, read_count.reshape(1, 1),
    )


def solution(mesh):
    split = P(("dp", "ctx"), "tp")
    per_ctx = P(("dp", "ctx"), None)
    flat = P(("dp", "ctx"))
    return jax.shard_map(
        body,
        mesh=mesh,
        in_specs=(split,) * 6 + (flat, per_ctx, per_ctx, per_ctx, flat),
        out_specs=(split,) * 5,
        check_vma=False,
    )
```

profile of v0, /device:TPU:32, one launch (start us, length us, event | category | flops | bytes accessed | tf_op | source)
XLA Modules:
  0.0 98.8 jit_solution(15880119170262323712)
XLA Ops:
  1.3 0.0 copy-start.9
  1.3 0.0 copy-start.6
  1.3 0.0 copy-start.7
  1.3 0.0 copy-start.8
  1.3 0.6 copy-done.9
  1.9 0.0 copy-done.6
  2.0 0.0 copy-done.7
  2.0 0.0 copy-done.8
  2.0 0.0 copy-start
  2.0 1.0 %copy-done = bf16[128,2048]{1,0:T(8,128)(2,1)S(1)} copy-done((bf16[128,2048]{1,0:T(8,128)(2,1)S(1)}, bf16[128,2048]{1,0:T(8,128)(2,1)}, u32[]{:S(2)}) %copy-start) | copy-done | bytes 524312
  3.0 0.0 copy-start.1
  3.0 1.0 %copy-done.1 = bf16[128,2048]{1,0:T(8,128)(2,1)S(1)} copy-done((bf16[128,2048]{1,0:T(8,128)(2,1)S(1)}, bf16[128,2048]{1,0:T(8,128)(2,1)}, u32[]{:S(2)}) %copy-start.1) | copy-done | bytes 524312
  4.1 0.0 copy-start.2
  4.1 0.9 copy-done.2
  5.0 0.0 copy-start.3
  5.0 0.9 copy-done.3
  5.9 0.0 copy-start.4
  5.9 0.8 copy-done.4
  6.7 0.0 copy-start.5
  6.7 0.8 copy-done.5
  7.6 87.7 %tail_attention_backward.1 = (bf16[128,2048]{1,0:T(8,128)(2,1)S(1)}, bf16[128,256]{1,0:T(8,128)(2,1)S(1)}, bf16[128,256]{1,0:T(8,128)(2,1)S(1)}, f32[256,256]{1,0:T(8,128)S(1)}, f32[256,256]{1,0:T(8,128)S(1)}) custom-call(bf16[128,2048]{1,0:T(8,128)(2,1)S(1)} %copy-done, bf16[128,2048]{1,0:T(8,128)(2,1)S(1)} %copy-done.1, bf16[128,256]{1,0:T(8,128)(2,1)S(1)} %copy-done.4, ...), custom_call_target="tpu_custom_call" | custom-call | flops 15502147584 | bytes 4194304 | tf_op jit(solution)/shard_map/tail_attention_backward/pallas_call | solution.py:486
  95.3 0.8 copy.22
  96.1 0.6 copy.23
  96.7 0.6 copy.24
  97.3 0.7 copy.25
  98.0 0.7 copy.26
Async XLA Ops:
  1.3 0.7 copy-start.9
  1.3 0.7 copy-start.6
  1.3 0.7 copy-start.7
  1.3 0.7 copy-start.8
  2.0 1.0 %copy-start = (bf16[128,2048]{1,0:T(8,128)(2,1)S(1)}, bf16[128,2048]{1,0:T(8,128)(2,1)}, u32[]{:S(2)}) copy-start(bf16[128,2048]{1,0:T(8,128)(2,1)} %q_ref.1) | copy-start | bytes 1572868
  3.0 1.0 %copy-start.1 = (bf16[128,2048]{1,0:T(8,128)(2,1)S(1)}, bf16[128,2048]{1,0:T(8,128)(2,1)}, u32[]{:S(2)}) copy-start(bf16[128,2048]{1,0:T(8,128)(2,1)} %do_ref.1) | copy-start | bytes 1572868
  4.1 0.9 copy-start.2
  5.0 0.9 copy-start.3
  5.9 0.8 copy-start.4
  6.7 0.8 copy-start.5
where the time goes:
time: 101 us; the launch traced here: 98.8 us
  Pallas kernels  87.7 us (87%)
  local copies, waits for them, and re-layouts  9.7 us (10%)
  between operations  1.33 us (1%)
    pallas_call x1, Pallas kernels, body(): pl.pallas_call(kernel, name='tail_attention_backward', out_shape=(jax.Sha...  87.7 us
    unnamed x25, local copies, waits for them, and re-layouts  9.7 us

commit v1 on v0

v1 whole, which is shorter than its diff:
```python
import functools
import math

import jax
import jax.numpy as jnp
from jax import lax
from jax.experimental import pallas as pl
from jax.experimental.pallas import tpu as pltpu
from jax.sharding import PartitionSpec as P

W = 128
NX = 4
NZ = 4
SCALE = 1.0 / math.sqrt(W)
LOG2E = 1.4426950408889634
SCORE_TO_LOG2 = SCALE * LOG2E
MASKED = -1e30
FLOOR = -1e29
NB = 256
f32 = jnp.float32
bf16 = jnp.bfloat16
MESH = pl.DeviceIdType.MESH
TT = (((0,), (0,)), ((), ()))

GATHER = (
    (
        (("A000", "A001", "A002", "A010", "A011", "A012",), "A00"),
        ((), "A01"),
        (("A10w", "P00w", "M00w", "A100", "A101",), "A10"),
        ((), "P00"),
        ((), "M00"),
        (("A11w", "P01w", "M01w", "A110", "A111",), "A11"),
        ((), "P01"),
        ((), "M01"),
        (("A20w", "P10w", "M10w", "A200", "A201",), "A20"),
        ((), "P10"),
        ((), "M10"),
        (("A21w", "P11w", "M11w", "A210", "A211",), "A21"),
        ((), "P11"),
        ((), "M11"),
        (("A30w", "P20w", "M20w", "A300", "A301",), "A30"),
        ((), "P20"),
        ((), "M20"),
        (("A31w", "P21w", "M21w", "M000", "M100", "A310", "A311", "P011", "P111",), "A31"),
        ((), "P21"),
        ((), "M21"),
        (("C20w", "P30w", "M30w",), "C20"),
        ((), "P30"),
        ((), "M30"),
        (("C21w", "P31w", "M31w",), "C21"),
        ((), "P31"),
        ((), "M31"),
        (("C30w", "C00w", "C01w",), "C30"),
        ((), "C00"),
        ((), "C01"),
        (("C10w", "C31w", "C11w",), "C10"),
        ((), "C31"),
        ((), "C11"),
    ),
    (
        (("A002", "A000", "A001", "A003", "A012", "A010", "A011", "A013",), "A00"),
        ((), "A01"),
        (("A10w", "A20w", "P00w", "M00w", "A102", "M000", "A100", "A101", "A203",), "A10"),
        ((), "A20"),
        ((), "P00"),
        ((), "M00"),
        (("A11w", "A21w", "P01w", "M01w", "A201", "A112", "A110", "P011", "A111", "A213",), "A11"),
        ((), "A21"),
        ((), "P01"),
        ((), "M01"),
        (("A30w", "P10w", "C00w", "C002", "A303",), "A30"),
        ((), "P10"),
        ((), "C00"),
        (("M10w", "A31w", "C01w", "M100", "A200", "A300", "C012", "A210", "A310", "A313",), "M10"),
        ((), "A31"),
        ((), "C01"),
        (("C20w", "P11w", "M11w", "A301", "C203", "P111", "A211", "A311",), "C20"),
        ((), "P11"),
        ((), "M11"),
        (("P20w", "C10w", "C21w", "C102", "C213",), "P20"),
        ((), "C10"),
        ((), "C21"),
        (("M20w", "C11w", "C112",), "M20"),
        ((), "C11"),
        (("C30w", "C303",), "C30"),
        (("P21w", "M21w",), "P21"),
        ((), "M21"),
        (("C31w", "C313",), "C31"),
        (("P30w", "M30w",), "P30"),
        ((), "M30"),
        (("P31w", "M31w",), "P31"),
        ((), "M31"),
    ),
)
SCATTER = (
    (
        ("23", ()),
        ("m3", ()),
        ("21", ()),
        ("22", ()),
        ("p3", ()),
        ("p2", ()),
        ("m2", ()),
        ("p1", ("p11",)),
        ("01", ()),
        ("03", ("030",)),
        ("20", ()),
        ("m1", ("m10", "031",)),
        ("p0", ()),
        ("m0", ()),
        ("02", ("020",)),
        ("00", ()),
        ("T0", ("021",)),
        ("U0", ("m00", "011", "010", "p01", "000", "001",)),
    ),
    (
        ("m3", ()),
        ("p0", ()),
        ("p3", ()),
        ("m0", ()),
        ("23", ("230",)),
        ("21", ()),
        ("03", ()),
        ("01", ("231",)),
        ("p2", ("210",)),
        ("m1", ()),
        ("m2", ()),
        ("22", ("211", "220", "221",)),
        ("02", ("m10",)),
        ("p1", ()),
        ("20", ("030",)),
        ("00", ("200",)),
        ("T0", ("031",)),
        ("U0", ("p11", "201", "020", "021", "010", "011", "m00", "p01", "000", "001",)),
    ),
)


def kernel(
    q_hbm, do_hbm, tk_hbm, tv_hbm, kc_hbm, vc_hbm, rl_hbm, ro_hbm, rt_hbm, rs_hbm, rc_hbm,
    gq_hbm, gk_hbm, gv_hbm, gck_hbm, gcv_hbm,
    gq_ref, gk_ref, gv_ref, gck_ref, gcv_ref, tk_ref, tv_ref, rl_ref, ro_ref, rt_ref, rs_ref, rc_ref,
    G, GR, R1, R2, RZ2, RZ, QR, DR, QT, DT, m_ref, l_ref, c_ref, shift_ref, bias_ref, dq_ref, PS, DS, top_ref,
    in_sem, q_sem, out_sem, a_recv, a_send, r1_recv, r1_send, r2_recv, r2_send, rz2_recv, rz2_send, rz_recv, rz_send,
):
    me = lax.axis_index("ctx")
    x = me // NZ
    z = me % NZ
    xp = lax.rem(x + 1, NX)
    xm = lax.rem(x + NX - 1, NX)
    x2 = lax.rem(x + 2, NX)
    inner = (z == 1) | (z == 2)
    edge = (z == 0) | (z == 3)
    low = z < 2
    zi = jnp.where(low, z + 1, z - 1)
    zo = jnp.where(low, z - 1, z + 1)
    to = [xp * NZ + z, xm * NZ + z, x * NZ + zi, x * NZ + zo]
    zk = [z, jnp.where(lax.rem(z, 2) == 0, z + 1, z - 1), jnp.where(low, 2, 1), jnp.where(low, 3, 0)]
    column = {"A": x, "P": xp, "M": xm, "C": x2, "0": x, "p": xp, "m": xm, "2": x2}
    half = 8 * W // NB

    def owner_of(group, k):
        return column[group] * NZ + zk[k]

    def by_class(ends, middle):
        pl.when(edge)(ends)
        pl.when(inner)(middle)

    def pick(n, lo, hi, leaf):
        if hi - lo == 1:
            return leaf(lo)
        mid = (lo + hi) // 2
        return lax.cond(n < mid, lambda: pick(n, lo, mid, leaf), lambda: pick(n, mid, hi, leaf))

    def send(src, dst, ssem, rsem, dev):
        pltpu.make_async_remote_copy(
            src_ref=src, dst_ref=dst, send_sem=ssem, recv_sem=rsem, device_id={"ctx": dev}, device_id_type=MESH
        ).start()

    def wait_recv(dst, rsem):
        pltpu.make_async_remote_copy(
            src_ref=dst, dst_ref=dst, send_sem=rsem, recv_sem=rsem, device_id={"ctx": to[0]}, device_id_type=MESH
        ).wait_recv()

    def wait_send(ssem):
        pltpu.make_async_remote_copy(
            src_ref=G.at[0, 0], dst_ref=G.at[0, 0], send_sem=ssem, recv_sem=ssem, device_id={"ctx": to[0]},
            device_id_type=MESH,
        ).wait_send()

    own = [
        pltpu.make_async_copy(kc_hbm, G.at[me, :, 0], in_sem.at[0]),
        pltpu.make_async_copy(vc_hbm, G.at[me, :, 1], in_sem.at[1]),
    ]
    rest = [
        pltpu.make_async_copy(src, dst, in_sem.at[i + 2])
        for i, (src, dst) in enumerate(
            (
                (tk_hbm, tk_ref), (tv_hbm, tv_ref), (rl_hbm, rl_ref),
                (ro_hbm, ro_ref), (rt_hbm, rt_ref), (rs_hbm, rs_ref), (rc_hbm, rc_ref),
            )
        )
    ]
    rest += [
        pltpu.make_async_copy(src.at[:, pl.ds(i * W, W)], dst.at[i // 8, pl.ds(i % 8 * W, W)], q_sem.at[n, i])
        for i in range(16)
        for n, (src, dst) in enumerate(((q_hbm, QR), (do_hbm, DR)))
    ]
    for copy in own + rest:
        copy.start()

    barrier = pltpu.get_barrier_semaphore()

    def greet(dev):
        pl.semaphore_signal(barrier, inc=1, device_id={"ctx": dev}, device_id_type=MESH)

    for d in range(3):
        greet(to[d])
    pl.when(inner)(lambda: greet(to[3]))
    for copy in own:
        copy.wait()
    by_class(lambda: pl.semaphore_wait(barrier, 3), lambda: pl.semaphore_wait(barrier, 4))

    def gather_op(op):
        group, k, a = op[0], int(op[1]), int(op[2])
        owner = owner_of(group, k)
        tile = G.at[owner, a]
        if op[3] == "w":
            wait_recv(tile, a_recv.at[owner, a])
        else:
            d = int(op[3])
            send(tile, tile, a_send.at[d, 0 if group == "A" else 1, k, a], a_recv.at[owner, a], to[d])

    def gather_ops(cls, n):
        for op in GATHER[cls][n][0]:
            gather_op(op)

    by_class(lambda: gather_ops(0, 0), lambda: gather_ops(1, 0))

    for copy in rest:
        copy.wait()
    for h in range(2):
        for j in range(8):
            rows = slice(j * W, (j + 1) * W)
            QT[h, :, rows] = QR[h, rows, :].T
            DT[h, :, rows] = DR[h, rows, :].T
    reads = ro_ref.shape[1]
    tid = ro_ref[...] * 2 + rt_ref[...]
    live = lax.broadcasted_iota(jnp.int32, (1, reads), 1) < rc_ref[0]
    tid = jnp.where(live, tid, -1)
    named = lax.broadcasted_iota(jnp.int32, (2 * NX * NZ, reads), 0) == tid
    count0 = jnp.sum(jnp.where(named & (rs_ref[...] == 0), 1.0, 0.0), axis=1, keepdims=True)
    count1 = jnp.sum(jnp.where(named & (rs_ref[...] == 1), 1.0, 0.0), axis=1, keepdims=True)
    rl = rl_ref[...]
    times = jnp.where(rl == 0, count0, count1)
    bias_ref[...] = jnp.where(times > 0.5, jnp.log2(jnp.maximum(times, 1.0)), MASKED)
    cut = jnp.sum(jnp.where(rl == 0, 1.0, 0.0), axis=1, keepdims=True)
    key_at = lax.broadcasted_iota(jnp.int32, (W, W), 0)
    row_at = lax.broadcasted_iota(jnp.int32, (W, W), 1)
    tail_ok = (key_at <= row_at) & jnp.logical_not((key_at.astype(f32) < cut) & (row_at.astype(f32) >= cut))
    tail_ok = jnp.concatenate([tail_ok.astype(f32)] * (NB // W), axis=1) > 0.5

    for h in range(2):
        hs = slice(h * W, (h + 1) * W)
        for j in range(half):
            sl = slice(j * NB, (j + 1) * NB)
            s = jnp.dot(tk_ref[:, hs], QT[h, :, sl], preferred_element_type=f32)
            dp = jnp.dot(tv_ref[:, hs], DT[h, :, sl], preferred_element_type=f32)
            t = jnp.where(tail_ok, s * SCORE_TO_LOG2, MASKED).reshape(16, 8, NB)
            top = jnp.maximum(jnp.max(t, axis=0), FLOOR)
            e = jnp.exp2(t - top[None])
            low_sum = jnp.sum(e, axis=0)
            cross = jnp.sum(e * dp.reshape(16, 8, NB), axis=0)
            part = jnp.exp2(top - jnp.max(top, axis=0, keepdims=True))
            mean = jnp.sum(cross * part, axis=0, keepdims=True) / jnp.sum(low_sum * part, axis=0, keepdims=True)
            mean = jnp.broadcast_to(mean, (8, NB))
            m_ref[h, :, sl] = top
            l_ref[h, :, sl] = low_sum
            c_ref[h, :, sl] = cross - mean * low_sum
            shift_ref[h, :, sl] = mean

    def stats_tile(owner, a):
        b = jnp.broadcast_to(bias_ref[pl.ds(owner * 2 + a, 1), :], (8, W))
        b = jnp.concatenate([b] * (NB // W), axis=1)
        for h in range(2):
            hs = slice(h * W, (h + 1) * W)
            for j in range(half):
                sl = slice(j * NB, (j + 1) * NB)
                s = jnp.dot(G[owner, a, 0, :, hs], QT[h, :, sl], preferred_element_type=f32)
                dp = jnp.dot(G[owner, a, 1, :, hs], DT[h, :, sl], preferred_element_type=f32)
                t = (s * SCORE_TO_LOG2).reshape(16, 8, NB)
                old = m_ref[h, :, sl]
                new = jnp.maximum(old, jnp.max(t, axis=0) + b)
                fade = jnp.exp2(old - new)
                e = jnp.exp2(t - (new - b)[None])
                dlow = (dp.reshape(16, 8, NB) - shift_ref[h, :, sl][None]).astype(bf16)
                PS[owner, h, a, :, sl] = e.reshape(W, NB).astype(bf16)
                DS[owner, h, a, :, sl] = dlow.reshape(W, NB)
                top_ref[owner, a, h, :, sl] = new
                m_ref[h, :, sl] = new
                l_ref[h, :, sl] = l_ref[h, :, sl] * fade + jnp.sum(e, axis=0)
                c_ref[h, :, sl] = c_ref[h, :, sl] * fade + jnp.sum(e * dlow.astype(f32), axis=0)

    def gather_leaf(cls):
        def leaf(n):
            if n > 0:
                gather_ops(cls, n)
            op = GATHER[cls][n][1]
            return owner_of(op[0], int(op[1])) * 2 + int(op[2])

        return leaf

    def gather_step(n, carry):
        at = lax.cond(
            inner, lambda: pick(n, 0, 2 * NX * NZ, gather_leaf(1)), lambda: pick(n, 0, 2 * NX * NZ, gather_leaf(0))
        )
        stats_tile(at // 2, at % 2)
        return carry

    lax.fori_loop(0, 2 * NX * NZ, gather_step, 0)

    for h in range(2):
        m = m_ref[h]
        top = jnp.max(m, axis=0, keepdims=True)
        part = jnp.exp2(m - top)
        total = jnp.sum(l_ref[h] * part, axis=0, keepdims=True)
        cross = jnp.sum(c_ref[h] * part, axis=0, keepdims=True)
        m_ref[h] = jnp.broadcast_to(top + jnp.log2(total), (8, 8 * W))
        c_ref[h] = jnp.broadcast_to(cross / total, (8, 8 * W))
        dq_ref[h] = jnp.zeros((W, 8 * W), f32)

    def grads_chunk(owner):
        for h in range(2):
            hs = slice(h * W, (h + 1) * W)
            for a in range(2):
                for j in range(half):
                    sl = slice(j * NB, (j + 1) * NB)
                    f = jnp.exp2(top_ref[owner, a, h, :, sl] - m_ref[h, :, sl])
                    p = PS[owner, h, a, :, sl].astype(f32).reshape(16, 8, NB) * f[None]
                    d = p * (DS[owner, h, a, :, sl].astype(f32).reshape(16, 8, NB) - c_ref[h, :, sl][None])
                    PS[owner, h, a, :, sl] = p.reshape(W, NB).astype(bf16)
                    DS[owner, h, a, :, sl] = d.reshape(W, NB).astype(bf16)
            d_all = DS[owner, h].reshape(2 * W, 8 * W)
            keys = jnp.concatenate([G[owner, 0, 0, :, hs], G[owner, 1, 0, :, hs]], axis=0)
            dq_ref[h] += lax.dot_general(keys, d_all, TT, preferred_element_type=f32)
            dv = jnp.dot(PS[owner, h].reshape(2 * W, 8 * W), DR[h], preferred_element_type=f32)
            dk = jnp.dot(d_all, QR[h], preferred_element_type=f32) * SCALE
            for a in range(2):
                rows = slice(a * W, (a + 1) * W)
                GR[owner, a, 0, :, hs] = dk[rows].astype(bf16)
                GR[owner, a, 1, :, hs] = dv[rows].astype(bf16)

    def merge(ref, parts):
        def rows_of(i, carry):
            r = pl.ds(pl.multiple_of(i * 32, 32), 32)
            total = ref[:, r, :].astype(f32)
            for part in parts:
                total = total + part[:, r, :].astype(f32)
            ref[:, r, :] = total.astype(bf16)
            return carry

        lax.fori_loop(0, W // 32, rows_of, 0)

    def route(cls, group, k, a):
        needs = []
        if group == "2":
            if cls:
                needs.append((RZ2.at[k, a], rz2_recv.at[k, a]))
            if k >= 2:
                slot = k - 2 if cls else k
                return needs, 2, rz2_send.at[k - 2, a], RZ2.at[slot, a], rz2_recv.at[slot, a]
            return needs, 1 - a, r2_send.at[k, a], R2.at[k, a], r2_recv.at[k, a]
        if group in "mp":
            d = "mp".index(group)
            if k < 2 and a == d:
                needs.append((R2.at[k, a], r2_recv.at[k, a]))
            return needs, 1 - d, r1_send.at[d, k, a], R1.at[d, k, a], r1_recv.at[d, k, a]
        needs += [(R1.at[d, k, a], r1_recv.at[d, k, a]) for d in range(2)]
        if k == 0:
            needs += [(RZ.at[slot, a], rz_recv.at[slot, a]) for slot in ((0, 4) if cls else (0,))]
            return needs, None, None, None, None
        if cls:
            needs.append((RZ.at[k, a], rz_recv.at[k, a]))
            slot = 0 if k == 1 else k - 2
        else:
            slot = 4 if k == 1 else k
        return needs, 3 if cls and k == 1 else 2, rz_send.at[k - 1, a], RZ.at[slot, a], rz_recv.at[slot, a]

    def pass_on(cls, group, k, a):
        owner = owner_of(group, k)
        needs, d, ssem, there, rsem = route(cls, group, k, a)
        for ref, sem in needs:
            wait_recv(ref, sem)
        if d is None:
            rows = slice(a * W, (a + 1) * W)
            for i, out in enumerate((gck_ref, gcv_ref)):
                total = GR[owner, a, i].astype(f32)
                for ref, _ in needs:
                    total = total + ref[i].astype(f32)
                out[rows, :] = total
            return
        if needs:
            merge(GR.at[owner, a], [ref for ref, _ in needs])
        send(GR.at[owner, a], there, ssem, rsem, to[d])

    def after_chunk(cls, n):
        chunk, posts = SCATTER[cls][n]
        if chunk[0] not in "TU":
            for a in range(2):
                if not route(cls, chunk[0], int(chunk[1]), a)[0]:
                    pass_on(cls, chunk[0], int(chunk[1]), a)
        for post in posts:
            pass_on(cls, post[0], int(post[1]), int(post[2]))

    def chunk_leaf(cls):
        return lambda n: owner_of(SCATTER[cls][n][0][0], int(SCATTER[cls][n][0][1]))

    def after_leaf(cls):
        def leaf(n):
            after_chunk(cls, n)

        return leaf

    def scatter_step(n, carry):
        owner = lax.cond(
            inner, lambda: pick(n, 0, NX * NZ, chunk_leaf(1)), lambda: pick(n, 0, NX * NZ, chunk_leaf(0))
        )
        grads_chunk(owner)
        by_class(lambda: pick(n, 0, NX * NZ, after_leaf(0)), lambda: pick(n, 0, NX * NZ, after_leaf(1)))
        return carry

    lax.fori_loop(0, NX * NZ, scatter_step, 0)

    for h in range(2):
        hs = slice(h * W, (h + 1) * W)
        for j in range(half):
            sl = slice(j * NB, (j + 1) * NB)
            s = jnp.dot(tk_ref[:, hs], QT[h, :, sl], preferred_element_type=f32)
            dp = jnp.dot(tv_ref[:, hs], DT[h, :, sl], preferred_element_type=f32)
            t = jnp.where(tail_ok, s * SCORE_TO_LOG2, MASKED).reshape(16, 8, NB)
            p = jnp.exp2(t - m_ref[h, :, sl][None])
            d = p * (dp.reshape(16, 8, NB) - (c_ref[h, :, sl] + shift_ref[h, :, sl])[None])
            PS[0, h, 0, :, sl] = p.reshape(W, NB).astype(bf16)
            DS[0, h, 0, :, sl] = d.reshape(W, NB).astype(bf16)
        gv_ref[:, hs] = jnp.dot(PS[0, h, 0], DR[h], preferred_element_type=f32).astype(bf16)
        gk_ref[:, hs] = (jnp.dot(DS[0, h, 0], QR[h], preferred_element_type=f32) * SCALE).astype(bf16)
        dq_ref[h] += lax.dot_general(tk_ref[:, hs], DS[0, h, 0], TT, preferred_element_type=f32)
    by_class(lambda: after_chunk(0, NX * NZ), lambda: after_chunk(1, NX * NZ))
    for h in range(2):
        for j in range(8):
            gq_ref[:, (h * 8 + j) * W : (h * 8 + j + 1) * W] = (
                (dq_ref[h, :, j * W : (j + 1) * W] * SCALE).T.astype(bf16)
            )
    results = [
        pltpu.make_async_copy(src, dst, out_sem.at[i])
        for i, (src, dst) in enumerate(
            (
                (gq_ref, gq_hbm), (gk_ref, gk_hbm), (gv_ref, gv_hbm), (gck_ref, gck_hbm), (gcv_ref, gcv_hbm),
            )
        )
    ]
    for copy in results[:3]:
        copy.start()
    by_class(lambda: after_chunk(0, NX * NZ + 1), lambda: after_chunk(1, NX * NZ + 1))

    for copy in results[3:]:
        copy.start()

    def sums_left(cls):
        for group in "2mp0":
            for k in range(4):
                for a in range(2):
                    if group + str(k) != "00":
                        wait_send(route(cls, group, k, a)[2])

    def gather_left(cls):
        for ops, _ in GATHER[cls]:
            for op in ops:
                if op[3] != "w":
                    wait_send(a_send.at[int(op[3]), 0 if op[0] == "A" else 1, int(op[1]), int(op[2])])

    by_class(lambda: gather_left(0), lambda: gather_left(1))

    by_class(lambda: sums_left(0), lambda: sums_left(1))
    for copy in results:
        copy.wait()


def write_out(*refs):
    n = len(refs) // 2
    sem = refs[-1]
    copies = [pltpu.make_async_copy(refs[i], refs[n + i], sem.at[i]) for i in range(n)]
    for copy in copies:
        copy.start()
    for copy in copies:
        copy.wait()


def body(q, do, tk, tv, kc, vc, row_list, read_owner, read_tile, read_list, read_count):
    rows, width = q.shape
    kv_width = tk.shape[1]
    groups = width // kv_width
    reads = read_owner.shape[1]
    owners = NX * NZ
    hbm = pl.BlockSpec(memory_space=pltpu.HBM)
    tile = (2, W, kv_width)
    lanes = groups * W
    dma = pltpu.SemaphoreType.DMA
    scratch = [
        pltpu.VMEM((rows, width), bf16),
        pltpu.VMEM((rows, kv_width), bf16),
        pltpu.VMEM((rows, kv_width), bf16),
        pltpu.VMEM(kc.shape, f32),
        pltpu.VMEM(vc.shape, f32),
        pltpu.VMEM((rows, kv_width), bf16),
        pltpu.VMEM((rows, kv_width), bf16),
        pltpu.VMEM((1, rows), jnp.int32),
        pltpu.VMEM((1, reads), jnp.int32),
        pltpu.VMEM((1, reads), jnp.int32),
        pltpu.VMEM((1, reads), jnp.int32),
        pltpu.SMEM((1,), jnp.int32),
        pltpu.VMEM((owners, 2) + tile, bf16),
        pltpu.VMEM((owners, 2) + tile, bf16),
        pltpu.VMEM((2, 4, 2) + tile, bf16),
        pltpu.VMEM((2, 2) + tile, bf16),
        pltpu.VMEM((4, 2) + tile, bf16),
        pltpu.VMEM((5, 2) + tile, bf16),
        pltpu.VMEM((2, lanes, W), bf16),
        pltpu.VMEM((2, lanes, W), bf16),
        pltpu.VMEM((2, W, lanes), bf16),
        pltpu.VMEM((2, W, lanes), bf16),
        pltpu.VMEM((2, 8, lanes), f32),
        pltpu.VMEM((2, 8, lanes), f32),
        pltpu.VMEM((2, 8, lanes), f32),
        pltpu.VMEM((2, 8, lanes), f32),
        pltpu.VMEM((2 * owners, W), f32),
        pltpu.VMEM((2, W, lanes), f32),
        pltpu.VMEM((owners, 2, 2, W, lanes), bf16),
        pltpu.VMEM((owners, 2, 2, W, lanes), bf16),
        pltpu.VMEM((owners, 2, 2, 8, lanes), f32),
        dma((9,)),
        dma((2, 16)),
        dma((5,)),
        dma((owners, 2)),
        dma((4, 2, 4, 2)),
        dma((2, 4, 2)),
        dma((2, 4, 2)),
        dma((2, 2)),
        dma((2, 2)),
        dma((4, 2)),
        dma((2, 2)),
        dma((5, 2)),
        dma((3, 2)),
    ]
    pairs = 2 * groups * rows * (2 * owners + 1) * W * W * 2
    shapes = (
        jax.ShapeDtypeStruct((rows, width), bf16),
        jax.ShapeDtypeStruct((rows, kv_width), bf16),
        jax.ShapeDtypeStruct((rows, kv_width), bf16),
        jax.ShapeDtypeStruct(kc.shape, f32),
        jax.ShapeDtypeStruct(vc.shape, f32),
    )
    results = pl.pallas_call(
        kernel,
        name="tail_attention_backward",
        out_shape=shapes,
        in_specs=[hbm] * 11,
        out_specs=(hbm,) * 5,
        scratch_shapes=scratch,
        cost_estimate=pl.CostEstimate(flops=5 * pairs, bytes_accessed=4 << 20, transcendentals=pairs // W),
        compiler_params=pltpu.CompilerParams(collective_id=0, has_side_effects=True, vmem_limit_bytes=60 << 20),
    )(
        q, do, tk, tv, kc.reshape(2, W, kv_width), vc.reshape(2, W, kv_width),
        row_list.reshape(1, rows), read_owner, read_tile, read_list, read_count,
    )
    return pl.pallas_call(
        write_out,
        name="write_out",
        out_shape=shapes,
        in_specs=[pl.BlockSpec(memory_space=pltpu.VMEM)] * 5,
        out_specs=(hbm,) * 5,
        scratch_shapes=[dma((5,))],
        compiler_params=pltpu.CompilerParams(vmem_limit_bytes=60 << 20),
    )(*results)


def solution(mesh):
    split = P(("dp", "ctx"), "tp")
    per_ctx = P(("dp", "ctx"), None)
    flat = P(("dp", "ctx"))
    return jax.shard_map(
        body,
        mesh=mesh,
        in_specs=(split,) * 6 + (flat, per_ctx, per_ctx, per_ctx, flat),
        out_specs=(split,) * 5,
        check_vma=False,
    )
```

time: 101 us -> 82.1 us (0.81); the launches traced: 98.8 us -> 81.9 us
  local copies, waits for them, and re-layouts: 9.7 us -> 0 us
  Pallas kernels: 87.7 us -> 80.6 us
    unnamed x25 -> x0, local copies, waits for them, and re-layouts: 9.7 us -> none
    pallas_call x1 -> x2, Pallas kernels: 87.7 us -> 80.6 us  [the longest x1 78.3 us: body(): pl.pallas_call(kernel, name='tail_attention_backward', out_shape=shapes,...]
where the time goes in v1:
time: 82.1 us; the launch traced here: 81.9 us
  Pallas kernels  80.6 us (98%)
  between operations  1.29 us (2%)
    pallas_call x1, Pallas kernels, body(): pl.pallas_call(kernel, name='tail_attention_backward', out_shape=shapes,...  78.3 us
    pallas_call x1, Pallas kernels, body(): pl.pallas_call(write_out, name='write_out', out_shape=shapes, in_specs=[p...  2.29 us

profile of v1, /device:TPU:32, one launch (start us, length us, event | category | flops | bytes accessed | tf_op | source)
XLA Modules:
  0.0 81.9 jit_solution(9157918784852514350)
XLA Ops:
  1.3 78.3 %tail_attention_backward.1 = (bf16[128,2048]{1,0:T(8,128)(2,1)}, bf16[128,256]{1,0:T(8,128)(2,1)}, bf16[128,256]{1,0:T(8,128)(2,1)}, f32[256,256]{1,0:T(8,128)}, f32[256,256]{1,0:T(8,128)}) custom-call(bf16[128,2048]{1,0:T(8,128)(2,1)} %q_hbm.1, bf16[128,2048]{1,0:T(8,128)(2,1)} %do_hbm.1, bf16[128,256]{1,0:T(8,128)(2,1)} %tk_hbm.1, ...), custom_call_target="tpu_custom_call" | custom-call | flops 11072962560 | bytes 4194304 | tf_op jit(solution)/shard_map/tail_attention_backward/pallas_call | solution.py:563
  79.6 2.3 %write_out.1 = (bf16[128,2048]{1,0:T(8,128)(2,1)}, bf16[128,256]{1,0:T(8,128)(2,1)}, bf16[128,256]{1,0:T(8,128)(2,1)}, f32[256,256]{1,0:T(8,128)}, f32[256,256]{1,0:T(8,128)}) custom-call(bf16[128,2048]{1,0:T(8,128)(2,1)} %get-tuple-element.10.refs_0_, bf16[128,256]{1,0:T(8,128)(2,1)} %get-tuple-element.11.refs_1_, ...), custom_call_target="tpu_custom_call" | custom-call | tf_op jit(solution)/shard_map/write_out/pallas_call | solution.py:576

commit v2 on v1

--- a/solution.py
+++ b/solution.py
@@ -138,10 +138,10 @@
 
 def kernel(
     q_hbm, do_hbm, tk_hbm, tv_hbm, kc_hbm, vc_hbm, rl_hbm, ro_hbm, rt_hbm, rs_hbm, rc_hbm,
-    gq_hbm, gk_hbm, gv_hbm, gck_hbm, gcv_hbm,
-    gq_ref, gk_ref, gv_ref, gck_ref, gcv_ref, tk_ref, tv_ref, rl_ref, ro_ref, rt_ref, rs_ref, rc_ref,
+    gq_ref, gk_ref, gv_ref, gck_ref, gcv_ref,
+    tk_ref, tv_ref, rl_ref, ro_ref, rt_ref, rs_ref, rc_ref,
     G, GR, R1, R2, RZ2, RZ, QR, DR, QT, DT, m_ref, l_ref, c_ref, shift_ref, bias_ref, dq_ref, PS, DS, top_ref,
-    in_sem, q_sem, out_sem, a_recv, a_send, r1_recv, r1_send, r2_recv, r2_send, rz2_recv, rz2_send, rz_recv, rz_send,
+    in_sem, q_sem, a_recv, a_send, r1_recv, r1_send, r2_recv, r2_send, rz2_recv, rz2_send, rz_recv, rz_send,
 ):
     me = lax.axis_index("ctx")
     x = me // NZ
@@ -451,20 +451,7 @@
             gq_ref[:, (h * 8 + j) * W : (h * 8 + j + 1) * W] = (
                 (dq_ref[h, :, j * W : (j + 1) * W] * SCALE).T.astype(bf16)
             )
-    results = [
-        pltpu.make_async_copy(src, dst, out_sem.at[i])
-        for i, (src, dst) in enumerate(
-            (
-                (gq_ref, gq_hbm), (gk_ref, gk_hbm), (gv_ref, gv_hbm), (gck_ref, gck_hbm), (gcv_ref, gcv_hbm),
-            )
-        )
-    ]
-    for copy in results[:3]:
-        copy.start()
     by_class(lambda: after_chunk(0, NX * NZ + 1), lambda: after_chunk(1, NX * NZ + 1))
-
-    for copy in results[3:]:
-        copy.start()
 
     def sums_left(cls):
         for group in "2mp0":
@@ -482,8 +469,6 @@
     by_class(lambda: gather_left(0), lambda: gather_left(1))
 
     by_class(lambda: sums_left(0), lambda: sums_left(1))
-    for copy in results:
-        copy.wait()
 
 
 def write_out(*refs):
@@ -502,16 +487,12 @@
     groups = width // kv_width
     reads = read_owner.shape[1]
     owners = NX * NZ
-    hbm = pl.BlockSpec(memory_space=pltpu.HBM)
+    vmem = pl.BlockSpec(memory_space=pltpu.VMEM)
+    hbm = pl.BlockSpec(memory_space=pl.ANY)
     tile = (2, W, kv_width)
     lanes = groups * W
     dma = pltpu.SemaphoreType.DMA
     scratch = [
-        pltpu.VMEM((rows, width), bf16),
-        pltpu.VMEM((rows, kv_width), bf16),
-        pltpu.VMEM((rows, kv_width), bf16),
-        pltpu.VMEM(kc.shape, f32),
-        pltpu.VMEM(vc.shape, f32),
         pltpu.VMEM((rows, kv_width), bf16),
         pltpu.VMEM((rows, kv_width), bf16),
         pltpu.VMEM((1, rows), jnp.int32),
@@ -540,7 +521,6 @@
         pltpu.VMEM((owners, 2, 2, 8, lanes), f32),
         dma((9,)),
         dma((2, 16)),
-        dma((5,)),
         dma((owners, 2)),
         dma((4, 2, 4, 2)),
         dma((2, 4, 2)),
@@ -565,7 +545,7 @@
         name="tail_attention_backward",
         out_shape=shapes,
         in_specs=[hbm] * 11,
-        out_specs=(hbm,) * 5,
+        out_specs=(vmem,) * 5,
         scratch_shapes=scratch,
         cost_estimate=pl.CostEstimate(flops=5 * pairs, bytes_accessed=4 << 20, transcendentals=pairs // W),
         compiler_params=pltpu.CompilerParams(collective_id=0, has_side_effects=True, vmem_limit_bytes=60 << 20),
@@ -577,7 +557,7 @@
         write_out,
         name="write_out",
         out_shape=shapes,
-        in_specs=[pl.BlockSpec(memory_space=pltpu.VMEM)] * 5,
+        in_specs=[vmem] * 5,
         out_specs=(hbm,) * 5,
         scratch_shapes=[dma((5,))],
         compiler_params=pltpu.CompilerParams(vmem_limit_bytes=60 << 20),

time: 82.1 us -> 82.3 us (level)
  no operation moved by 1% of the time
where the time goes in v2:
time: 82.3 us; the launch traced here: 82.2 us
  Pallas kernels  80.9 us (98%)
  between operations  1.29 us (2%)
    pallas_call x1, Pallas kernels, body(): pl.pallas_call(kernel, name='tail_attention_backward', out_shape=shapes,...  78.6 us
    pallas_call x1, Pallas kernels, body(): pl.pallas_call(write_out, name='write_out', out_shape=shapes, in_specs=[v...  2.29 us

profile of v2, /device:TPU:32, one launch (start us, length us, event | category | flops | bytes accessed | tf_op | source)
XLA Modules:
  0.0 82.2 jit_solution(4424316543983007753)
XLA Ops:
  1.3 78.6 %tail_attention_backward.1 = (bf16[128,2048]{1,0:T(8,128)(2,1)}, bf16[128,256]{1,0:T(8,128)(2,1)}, bf16[128,256]{1,0:T(8,128)(2,1)}, f32[256,256]{1,0:T(8,128)}, f32[256,256]{1,0:T(8,128)}) custom-call(bf16[128,2048]{1,0:T(8,128)(2,1)} %q_hbm.1, bf16[128,2048]{1,0:T(8,128)(2,1)} %do_hbm.1, bf16[128,256]{1,0:T(8,128)(2,1)} %tk_hbm.1, ...), custom_call_target="tpu_custom_call" | custom-call | flops 11072962560 | bytes 4194304 | tf_op jit(solution)/shard_map/tail_attention_backward/pallas_call | solution.py:543
  79.9 2.3 %write_out.1 = (bf16[128,2048]{1,0:T(8,128)(2,1)}, bf16[128,256]{1,0:T(8,128)(2,1)}, bf16[128,256]{1,0:T(8,128)(2,1)}, f32[256,256]{1,0:T(8,128)}, f32[256,256]{1,0:T(8,128)}) custom-call(bf16[128,2048]{1,0:T(8,128)(2,1)} %get-tuple-element.10.refs_0_, bf16[128,256]{1,0:T(8,128)(2,1)} %get-tuple-element.11.refs_1_, ...), custom_call_target="tpu_custom_call" | custom-call | tf_op jit(solution)/shard_map/write_out/pallas_call | solution.py:556

commit v3 on v2

--- a/solution.py
+++ b/solution.py
@@ -140,7 +140,7 @@
     q_hbm, do_hbm, tk_hbm, tv_hbm, kc_hbm, vc_hbm, rl_hbm, ro_hbm, rt_hbm, rs_hbm, rc_hbm,
     gq_ref, gk_ref, gv_ref, gck_ref, gcv_ref,
     tk_ref, tv_ref, rl_ref, ro_ref, rt_ref, rs_ref, rc_ref,
-    G, GR, R1, R2, RZ2, RZ, QR, DR, QT, DT, m_ref, l_ref, c_ref, shift_ref, bias_ref, dq_ref, PS, DS, top_ref,
+    G, R1, R2, RZ2, RZ, QR, DR, QT, DT, m_ref, l_ref, c_ref, shift_ref, bias_ref, dq_ref, PS, DS, top_ref,
     in_sem, q_sem, a_recv, a_send, r1_recv, r1_send, r2_recv, r2_send, rz2_recv, rz2_send, rz_recv, rz_send,
 ):
     me = lax.axis_index("ctx")
@@ -329,6 +329,14 @@
         c_ref[h] = jnp.broadcast_to(cross / total, (8, 8 * W))
         dq_ref[h] = jnp.zeros((W, 8 * W), f32)
 
+    def gather_left(cls):
+        for ops, _ in GATHER[cls]:
+            for op in ops:
+                if op[3] != "w":
+                    wait_send(a_send.at[int(op[3]), 0 if op[0] == "A" else 1, int(op[1]), int(op[2])])
+
+    by_class(lambda: gather_left(0), lambda: gather_left(1))
+
     def grads_chunk(owner):
         for h in range(2):
             hs = slice(h * W, (h + 1) * W)
@@ -347,8 +355,8 @@
             dk = jnp.dot(d_all, QR[h], preferred_element_type=f32) * SCALE
             for a in range(2):
                 rows = slice(a * W, (a + 1) * W)
-                GR[owner, a, 0, :, hs] = dk[rows].astype(bf16)
-                GR[owner, a, 1, :, hs] = dv[rows].astype(bf16)
+                G[owner, a, 0, :, hs] = dk[rows].astype(bf16)
+                G[owner, a, 1, :, hs] = dv[rows].astype(bf16)
 
     def merge(ref, parts):
         def rows_of(i, carry):
@@ -394,14 +402,14 @@
         if d is None:
             rows = slice(a * W, (a + 1) * W)
             for i, out in enumerate((gck_ref, gcv_ref)):
-                total = GR[owner, a, i].astype(f32)
+                total = G[owner, a, i].astype(f32)
                 for ref, _ in needs:
                     total = total + ref[i].astype(f32)
                 out[rows, :] = total
             return
         if needs:
-            merge(GR.at[owner, a], [ref for ref, _ in needs])
-        send(GR.at[owner, a], there, ssem, rsem, to[d])
+            merge(G.at[owner, a], [ref for ref, _ in needs])
+        send(G.at[owner, a], there, ssem, rsem, to[d])
 
     def after_chunk(cls, n):
         chunk, posts = SCATTER[cls][n]
@@ -460,13 +468,6 @@
                     if group + str(k) != "00":
                         wait_send(route(cls, group, k, a)[2])
 
-    def gather_left(cls):
-        for ops, _ in GATHER[cls]:
-            for op in ops:
-                if op[3] != "w":
-                    wait_send(a_send.at[int(op[3]), 0 if op[0] == "A" else 1, int(op[1]), int(op[2])])
-
-    by_class(lambda: gather_left(0), lambda: gather_left(1))
 
     by_class(lambda: sums_left(0), lambda: sums_left(1))
 
@@ -500,7 +501,6 @@
         pltpu.VMEM((1, reads), jnp.int32),
         pltpu.VMEM((1, reads), jnp.int32),
         pltpu.SMEM((1,), jnp.int32),
-        pltpu.VMEM((owners, 2) + tile, bf16),
         pltpu.VMEM((owners, 2) + tile, bf16),
         pltpu.VMEM((2, 4, 2) + tile, bf16),
         pltpu.VMEM((2, 2) + tile, bf16),
@@ -548,10 +548,16 @@
         out_specs=(vmem,) * 5,
         scratch_shapes=scratch,
         cost_estimate=pl.CostEstimate(flops=5 * pairs, bytes_accessed=4 << 20, transcendentals=pairs // W),
-        compiler_params=pltpu.CompilerParams(collective_id=0, has_side_effects=True, vmem_limit_bytes=60 << 20),
+        compiler_params=pltpu.CompilerParams(collective_id=0, has_side_effects=True, vmem_limit_bytes=50 << 20),
     )(
-        q, do, tk, tv, kc.reshape(2, W, kv_width), vc.reshape(2, W, kv_width),
-        row_list.reshape(1, rows), read_owner, read_tile, read_list, read_count,
+        *(
+            pltpu.with_memory_space_constraint(v, pltpu.HBM)
+            for v in (
+                q, do, tk, tv, kc.reshape(2, W, kv_width), vc.reshape(2, W, kv_width),
+                row_list.reshape(1, rows), read_owner, read_tile, read_list,
+            )
+        ),
+        read_count,
     )
     return pl.pallas_call(
         write_out,
@@ -560,7 +566,7 @@
         in_specs=[vmem] * 5,
         out_specs=(hbm,) * 5,
         scratch_shapes=[dma((5,))],
-        compiler_params=pltpu.CompilerParams(vmem_limit_bytes=60 << 20),
+        compiler_params=pltpu.CompilerParams(vmem_limit_bytes=2 << 20),
     )(*results)
 
 

time: 82.3 us -> 80.2 us (0.974)
  Pallas kernels: 80.9 us -> 78.8 us
    pallas_call x1, Pallas kernels: 2.29 us -> 1.05 us  [body(): pl.pallas_call(write_out, name='write_out', out_shape=shapes, in_specs=[v...]
    pallas_call x1, Pallas kernels: 78.6 us -> 77.7 us  [body(): pl.pallas_call(kernel, name='tail_attention_backward', out_shape=shapes,...]
where the time goes in v3:
time: 80.2 us; the launch traced here: 80.1 us
  Pallas kernels  78.8 us (98%)
  between operations  1.29 us (2%)
    pallas_call x1, Pallas kernels, body(): pl.pallas_call(kernel, name='tail_attention_backward', out_shape=shapes,...  77.7 us

profile of v3, /device:TPU:32, one launch (start us, length us, event | category | flops | bytes accessed | tf_op | source)
XLA Modules:
  0.0 80.1 jit_solution(7877927119792934566)
XLA Ops:
  1.3 77.7 %tail_attention_backward.1 = (bf16[128,2048]{1,0:T(8,128)(2,1)S(1)}, bf16[128,256]{1,0:T(8,128)(2,1)S(1)}, bf16[128,256]{1,0:T(8,128)(2,1)S(1)}, f32[256,256]{1,0:T(8,128)S(1)}, f32[256,256]{1,0:T(8,128)S(1)}) custom-call(bf16[128,2048]{1,0:T(8,128)(2,1)} %q_hbm.1, bf16[128,2048]{1,0:T(8,128)(2,1)} %do_hbm.1, bf16[128,256]{1,0:T(8,128)(2,1)} %tk_hbm.1, ...), custom_call_target="tpu_custom_call" | custom-call | flops 11072962560 | bytes 4194304 | tf_op jit(solution)/shard_map/tail_attention_backward/pallas_call | solution.py:543
  79.0 1.1 %write_out.1 = (bf16[128,2048]{1,0:T(8,128)(2,1)}, bf16[128,256]{1,0:T(8,128)(2,1)}, bf16[128,256]{1,0:T(8,128)(2,1)}, f32[256,256]{1,0:T(8,128)}, f32[256,256]{1,0:T(8,128)}) custom-call(bf16[128,2048]{1,0:T(8,128)(2,1)S(1)} %get-tuple-element.10.refs_0_, bf16[128,256]{1,0:T(8,128)(2,1)S(1)} %get-tuple-element.11.refs_1_, ...), custom_call_target="tpu_custom_call" | custom-call | tf_op jit(solution)/shard_map/write_out/pallas_call | solution.py:562

commit v4 on v3

--- a/solution.py
+++ b/solution.py
@@ -206,7 +206,7 @@
         for i in range(16)
         for n, (src, dst) in enumerate(((q_hbm, QR), (do_hbm, DR)))
     ]
-    for copy in own + rest:
+    for copy in own:
         copy.start()
 
     barrier = pltpu.get_barrier_semaphore()
@@ -217,6 +217,8 @@
     for d in range(3):
         greet(to[d])
     pl.when(inner)(lambda: greet(to[3]))
+    for copy in rest:
+        copy.start()
     for copy in own:
         copy.wait()
     by_class(lambda: pl.semaphore_wait(barrier, 3), lambda: pl.semaphore_wait(barrier, 4))

time: 80.2 us -> 80.1 us (level)
  no operation moved by 1% of the time
where the time goes in v4:
time: 80.1 us; the launch traced here: 80 us
  Pallas kernels  78.7 us (98%)
  between operations  1.29 us (2%)
    pallas_call x1, Pallas kernels, body(): pl.pallas_call(kernel, name='tail_attention_backward', out_shape=shapes,...  77.7 us

profile of v4, /device:TPU:32, one launch (start us, length us, event | category | flops | bytes accessed | tf_op | source)
XLA Modules:
  0.0 80.0 jit_solution(15175848412095097381)
XLA Ops:
  1.3 77.7 %tail_attention_backward.1 = (bf16[128,2048]{1,0:T(8,128)(2,1)S(1)}, bf16[128,256]{1,0:T(8,128)(2,1)S(1)}, bf16[128,256]{1,0:T(8,128)(2,1)S(1)}, f32[256,256]{1,0:T(8,128)S(1)}, f32[256,256]{1,0:T(8,128)S(1)}) custom-call(bf16[128,2048]{1,0:T(8,128)(2,1)} %q_hbm.1, bf16[128,2048]{1,0:T(8,128)(2,1)} %do_hbm.1, bf16[128,256]{1,0:T(8,128)(2,1)} %tk_hbm.1, ...), custom_call_target="tpu_custom_call" | custom-call | flops 11072962560 | bytes 4194304 | tf_op jit(solution)/shard_map/tail_attention_backward/pallas_call | solution.py:545
  79.0 1.1 %write_out.1 = (bf16[128,2048]{1,0:T(8,128)(2,1)}, bf16[128,256]{1,0:T(8,128)(2,1)}, bf16[128,256]{1,0:T(8,128)(2,1)}, f32[256,256]{1,0:T(8,128)}, f32[256,256]{1,0:T(8,128)}) custom-call(bf16[128,2048]{1,0:T(8,128)(2,1)S(1)} %get-tuple-element.10.refs_0_, bf16[128,256]{1,0:T(8,128)(2,1)S(1)} %get-tuple-element.11.refs_1_, ...), custom_call_target="tpu_custom_call" | custom-call | tf_op jit(solution)/shard_map/write_out/pallas_call | solution.py:564
